TPU v7x, 256 devices: a whole 4x4x8 slice. The times are simulated.
256 devices in a mesh: edge: 64 (over y, z, core), rep: 4 (over x).
Axes of the slice: x: 4, y: 4, z: 8, core: 2. Of those that a mesh axis runs over, the one named last changes fastest.
Arguments:
- entities: float32 [4, 65536, 400], P('rep', 'edge'), may hold values from -3 to 3
- ent_accum: float32 [4, 65536], P('rep', 'edge'), may hold values from 0.01 to 0.1
- relations: float32 [1000, 400], replicated, may hold values from -3 to 3
- rel_accum: float32 [1000], replicated, may hold values from 1 to 10
- heads: int32 [4, 2, 8192], P('rep', None, 'edge'), may hold values from 0 to 65535, as said below
- tails: int32 [4, 2, 8192], P('rep', None, 'edge'), may hold values from 0 to 65535, as said below
- negatives: int32 [4, 2, 65536], P('rep', None, 'edge'), may hold values from 0 to 65535, as said below
- rel_ids: int32 [4, 2, 8192], P('rep', None, 'edge'), may hold values from 0 to 999
Outputs:
- new_entities: float32 [4, 65536, 400], P('rep', 'edge')
- new_ent_accum: float32 [4, 65536], P('rep', 'edge')
- new_relations: float32 [1000, 400], replicated
- new_rel_accum: float32 [1000], replicated
Inputs may be any that keep to these rules, and one draw needn't show every extreme that they name: Row i of a bucket belongs to owner i // 1024. In each bucket, step and block, at most 40 of the block's 1280 requests (heads, tails, negatives together) name rows of one owner, and in every bucket and step one owner is named exactly 40 times by every block. `tails`: drawn together with heads under the same bound. `negatives`: drawn together with heads under the same bound.
All inputs are finite; a program needn't handle non-finite values.
Results may differ from a plain program's by a relative error of at most 0.0042.
Values may be sent and summed in bfloat16 or wider, within the bound.
No kernel may reach another device: no remote copies, remote signals or barrier semaphores. Data moves between devices by JAX's collectives and lax.ppermute only.
A program may use at most 64 MiB of HBM per device.

v0:
```python
import jax
import jax.numpy as jnp
from jax import lax
from jax.sharding import PartitionSpec as P

entity_rate = 0.1
relation_rate = 0.1


def complex_parts(rows):
    half = rows.shape[-1] // 2
    return (rows[:, :half], rows[:, half:])


def span_grads(head_entity_rows, tail_rows, negative_rows, relation_rows):
    negative_count = negative_rows.shape[0]
    head_full = head_entity_rows.astype(jnp.float32)
    tail_full = tail_rows.astype(jnp.float32)
    head_re, head_im = complex_parts(head_full)
    tail_re, tail_im = complex_parts(tail_full)
    rel_re, rel_im = complex_parts(relation_rows)
    query_tail = jnp.concatenate(
        [head_re * rel_re - head_im * rel_im, head_re * rel_im + head_im * rel_re], axis=1
    )
    query_head = jnp.concatenate(
        [rel_re * tail_re + rel_im * tail_im, rel_re * tail_im - rel_im * tail_re], axis=1
    )
    positive_score = jnp.sum(query_tail * tail_full, axis=1)
    tail_query16 = query_tail.astype(jnp.bfloat16)
    head_query16 = query_head.astype(jnp.bfloat16)
    contract_last = (((1,), (1,)), ((), ()))
    scores_tail = lax.dot_general(
        tail_query16, negative_rows, contract_last, preferred_element_type=jnp.float32
    )
    scores_head = lax.dot_general(
        head_query16, negative_rows, contract_last, preferred_element_type=jnp.float32
    )
    weight_tail = (jax.nn.sigmoid(scores_tail) / negative_count).astype(jnp.bfloat16)
    weight_head = (jax.nn.sigmoid(scores_head) / negative_count).astype(jnp.bfloat16)
    positive_weight = -jax.nn.sigmoid(-positive_score)[:, None]
    grad_tail_query = positive_weight * tail_full + jnp.dot(
        weight_tail, negative_rows, preferred_element_type=jnp.float32
    )
    grad_head_query = jnp.dot(weight_head, negative_rows, preferred_element_type=jnp.float32)
    contract_first = (((0,), (0,)), ((), ()))
    grad_negative = lax.dot_general(
        weight_tail, tail_query16, contract_first, preferred_element_type=jnp.float32
    )
    grad_negative = grad_negative + lax.dot_general(
        weight_head, head_query16, contract_first, preferred_element_type=jnp.float32
    )
    pull_re, pull_im = complex_parts(grad_tail_query)
    push_re, push_im = complex_parts(grad_head_query)
    grad_head = jnp.concatenate(
        [pull_re * rel_re + pull_im * rel_im, pull_im * rel_re - pull_re * rel_im], axis=1
    )
    grad_tail = positive_weight * query_tail + jnp.concatenate(
        [push_re * rel_re - push_im * rel_im, push_re * rel_im + push_im * rel_re], axis=1
    )
    grad_relation = jnp.concatenate(
        [
            pull_re * head_re + pull_im * head_im + push_re * tail_re + push_im * tail_im,
            pull_im * head_re - pull_re * head_im + push_re * tail_im - push_im * tail_re,
        ],
        axis=1,
    )
    return (jnp.concatenate([grad_head, grad_tail, grad_negative], axis=0), grad_relation)


def shards(entities, ent_accum, relations, rel_accum, heads, tails, negatives, rel_ids):
    owners_count = lax.axis_size("edge")
    rows_dev = entities.shape[1]
    width = entities.shape[2]
    span_size = heads.shape[2]
    request_count = 2 * span_size + negatives.shape[2]
    capacity = 2 * request_count // owners_count
    table = entities[0]
    accum = ent_accum[0]
    rel_table = relations
    rel_state = rel_accum
    for step_index in range(heads.shape[1]):
        requests = jnp.concatenate(
            [heads[0, step_index], tails[0, step_index], negatives[0, step_index]]
        )
        owner_ids = requests // rows_dev
        local_rows = requests % rows_dev
        order = jnp.argsort(owner_ids, stable=True)
        sorted_owner = owner_ids[order]
        counts = jnp.sum(
            (owner_ids[:, None] == jnp.arange(owners_count, dtype=jnp.int32)[None, :]).astype(
                jnp.int32
            ),
            axis=0,
        )
        starts = jnp.cumsum(counts) - counts
        ranks = jnp.arange(request_count, dtype=jnp.int32) - starts[sorted_owner]
        slot_of = jnp.zeros((request_count,), jnp.int32).at[order].set(ranks)
        flat_slot = owner_ids * capacity + slot_of
        send_rows = jnp.zeros((owners_count * capacity,), jnp.int32).at[flat_slot].set(local_rows)
        send_rows = send_rows.reshape(owners_count, capacity)
        received = lax.all_to_all(send_rows, "edge", split_axis=0, concat_axis=0, tiled=True)
        replies = lax.all_to_all(
            table[received].astype(jnp.bfloat16), "edge", split_axis=0, concat_axis=0, tiled=True
        )
        fetched = replies.reshape(owners_count * capacity, width)[flat_slot]
        relation_ids = rel_ids[0, step_index]
        request_grads, relation_grads = span_grads(
            fetched[:span_size],
            fetched[span_size : 2 * span_size],
            fetched[2 * span_size :],
            rel_table[relation_ids],
        )
        send_grads = (
            jnp.zeros((owners_count * capacity, width), jnp.bfloat16)
            .at[flat_slot]
            .set(request_grads.astype(jnp.bfloat16))
        )
        send_grads = send_grads.reshape(owners_count, capacity, width)
        returned = lax.all_to_all(send_grads, "edge", split_axis=0, concat_axis=0, tiled=True)
        entity_grad = jax.ops.segment_sum(
            returned.reshape(owners_count * capacity, width).astype(jnp.float32),
            received.reshape(owners_count * capacity),
            num_segments=rows_dev,
        )
        relation_local = jax.ops.segment_sum(
            relation_grads, relation_ids, num_segments=rel_table.shape[0]
        )
        relation_total = lax.psum(relation_local, ("edge", "rep"))
        accum = accum + jnp.mean(entity_grad * entity_grad, axis=1)
        table = table - entity_rate * entity_grad / jnp.sqrt(accum)[:, None]
        rel_state = rel_state + jnp.mean(relation_total * relation_total, axis=1)
        rel_table = rel_table - relation_rate * relation_total / jnp.sqrt(rel_state)[:, None]
    return (table[None], accum[None], rel_table, rel_state)


def solution(mesh):
    in_specs = (
        P("rep", "edge", None),
        P("rep", "edge"),
        P(),
        P(),
        P("rep", None, "edge"),
        P("rep", None, "edge"),
        P("rep", None, "edge"),
        P("rep", None, "edge"),
    )
    out_specs = (P("rep", "edge", None), P("rep", "edge"), P(), P())
    return jax.shard_map(shards, mesh=mesh, in_specs=in_specs, out_specs=out_specs, check_vma=False)
```

profile of v0, /device:TPU:14, one launch (start us, length us, event | category | flops | bytes accessed | tf_op | source)
XLA Modules:
  0.0 973.7 jit_solution(9696131635299519426)
XLA Ops:
  12.8 5.0 sort.31
  17.9 7.1 gather_fusion
  25.0 4.5 fusion.62
  30.4 35.7 %select_subtract_fusion.1 = s32[1280]{0:T(1024)S(1)} fusion(pred[1280]{0:T(1024)(128)(4,1)S(1)} %get-tuple-element.137, pred[1280]{0:T(1024)(128)(4,1)S(1)} %get-tuple-element.136, pred[1280]{0:T(1024)(128)(4,1)S(1)} %get-tuple-element.135, pred[1280]{0:T(1024)(128)(4,1)S(1)} %get-tuple-element.134, pred[1280]{0:T(1024)(128)(4,1)S(1)} %get-tuple-element.133, ...), kind=kLoop, calls=%fused_computation.273 | loop fusion | flops 74240 | bytes 83428 | tf_op jit(solution)/shard_map/sub | solution.py:96
  66.1 5.2 scatter_custom_fusion
  71.4 5.3 scatter_custom_fusion.1
  77.3 12.1 %all-to-all-start = ((s32[64,1,40]{2,1,0:T(1,128)}), s32[64,1,40]{2,1,0:T(1,128)S(1)}, u32[]{:S(2)}, u32[]{:S(2)}) async-start(s32[64,1,40]{2,1,0:T(1,128)} %bitcast.69), calls=%async_computation | async-start | bytes 65536 | tf_op jit(solution)/shard_map/all_to_all | solution.py:101
  91.3 6.7 all-to-all-done
  98.1 7.1 gather_fusion.1
  105.2 6.2 all-to-all-start.1
  111.4 5.0 sort.32
  116.5 7.1 gather_fusion.4
  125.4 4.3 fusion.63
  132.1 35.9 %select_subtract_fusion = s32[1280]{0:T(1024)S(1)} fusion(pred[1280]{0:T(1024)(128)(4,1)S(1)} %get-tuple-element.80, pred[1280]{0:T(1024)(128)(4,1)S(1)} %get-tuple-element.79, pred[1280]{0:T(1024)(128)(4,1)S(1)} %get-tuple-element.78, pred[1280]{0:T(1024)(128)(4,1)S(1)} %get-tuple-element.77, pred[1280]{0:T(1024)(128)(4,1)S(1)} %get-tuple-element.76, ...), kind=kLoop, calls=%fused_computation.272 | loop fusion | flops 74240 | bytes 83428 | tf_op jit(solution)/shard_map/sub | solution.py:96
  168.0 5.2 scatter_custom_fusion.4
  173.3 5.3 scatter_custom_fusion.5
  185.4 10.9 %all-to-all-start.3 = ((s32[64,1,40]{2,1,0:T(1,128)}), s32[64,1,40]{2,1,0:T(1,128)}, u32[]{:S(2)}, u32[]{:S(2)}) async-start(s32[64,1,40]{2,1,0:T(1,128)} %bitcast.146), calls=%async_computation.3 | async-start | bytes 65536 | tf_op jit(solution)/shard_map/all_to_all | solution.py:101
  196.3 4.7 gather_fusion.2
  206.3 10.0 %scatter_custom_fusion.2 = bf16[2560,400]{1,0:T(8,128)(2,1)} fusion(s32[1280]{0:T(1024)} %copy-done.14, bf16[1280,400]{1,0:T(8,128)(2,1)S(1)} %copy.75, bf16[]{:T(256)} %constant.79.clone.1), kind=kCustom, calls=%fused_computation.34 | custom fusion | bytes 2048512 | tf_op jit(solution)/shard_map/scatter | solution.py:116
  216.2 10.5 %all-to-all-start.2 = ((bf16[64,40,400]{2,1,0:T(8,128)(2,1)}), bf16[64,40,400]{2,1,0:T(8,128)(2,1)S(1)}, u32[]{:S(2)}, u32[]{:S(2)}) async-start(bf16[64,40,400]{2,1,0:T(8,128)(2,1)} %bitcast.75), calls=%async_computation.2 | async-start | bytes 5242880 | tf_op jit(solution)/shard_map/all_to_all | solution.py:119
  228.9 58.7 %all-to-all-done.2 = bf16[64,40,400]{2,1,0:T(8,128)(2,1)S(1)} async-done(((bf16[64,40,400]{2,1,0:T(8,128)(2,1)}), bf16[64,40,400]{2,1,0:T(8,128)(2,1)S(1)}, u32[]{:S(2)}, u32[]{:S(2)}) %all-to-all-start.2) | async-done | bytes 2048032 | tf_op jit(solution)/shard_map/all_to_all | solution.py:119
  289.1 17.8 %scatter_custom_fusion.3 = f32[1024,400]{1,0:T(8,128)S(1)} fusion(s32[2560]{0:T(1024)S(1)} %reshape.707, bf16[2560,400]{1,0:T(8,128)(2,1)} %bitcast.194, f32[]{:T(128)} %constant.68.clone.1), kind=kCustom, calls=%fused_computation.20 | custom fusion | flops 2048000 | bytes 3686404 | tf_op jit(solution)/shard_map/scatter-add | solution.py:120
  311.3 7.1 gather_fusion.5
  318.4 8.0 all-to-all-start.4
  329.5 277.9 %all-reduce.3.cloned.1.call-done = f32[1000,400]{1,0:T(8,128)} async-done(((f32[1000,400]{1,0:T(8,128)}), f32[1000,400]{1,0:T(8,128)}) %all-reduce.3.cloned.1.call-update) | async-done | bytes 1600016 | tf_op jit(solution)/shard_map/psum | solution.py:128
  609.6 3.3 divide_subtract_fusion.2
  615.7 6.9 gather_fusion.6
  631.6 10.6 %scatter_custom_fusion.7 = bf16[2560,400]{1,0:T(8,128)(2,1)} fusion(s32[1280]{0:T(1024)S(1)} %copy-done.16, bf16[1280,400]{1,0:T(8,128)(2,1)} %copy.84, bf16[]{:T(256)} %constant.79.clone.1), kind=kCustom, calls=%fused_computation.32 | custom fusion | bytes 2048512 | tf_op jit(solution)/shard_map/scatter | solution.py:116
  642.2 8.5 all-to-all-start.5
  655.3 276.0 %all-reduce.5.cloned.1.call-done = f32[1000,400]{1,0:T(8,128)} async-done(((f32[1000,400]{1,0:T(8,128)}), f32[1000,400]{1,0:T(8,128)}) %all-reduce.5.cloned.1.call-update) | async-done | bytes 1600016 | tf_op jit(solution)/shard_map/psum | solution.py:128
  933.8 3.3 divide_subtract_fusion.1
  939.9 19.2 %scatter_custom_fusion.8 = f32[1024,400]{1,0:T(8,128)} fusion(s32[2560]{0:T(1024)S(1)} %reshape.747, bf16[2560,400]{1,0:T(8,128)(2,1)} %bitcast.160, f32[]{:T(128)} %constant.68.clone.1), kind=kCustom, calls=%fused_computation.18 | custom fusion | flops 2048000 | bytes 3686404 | tf_op jit(solution)/shard_map/scatter-add | solution.py:120
  (166 shorter events, 67.5 us)
Async XLA Ops:
  71.4 114.0 %copy-start.14 = (s32[1280]{0:T(1024)}, s32[1280]{0:T(1024)S(1)}, u32[]{:S(2)}) copy-start(s32[1280]{0:T(1024)S(1)} %compare_select_fusion.6) | copy-start | bytes 15364
  77.3 20.6 %all-to-all-start = ((s32[64,1,40]{2,1,0:T(1,128)}), s32[64,1,40]{2,1,0:T(1,128)S(1)}, u32[]{:S(2)}, u32[]{:S(2)}) async-start(s32[64,1,40]{2,1,0:T(1,128)} %bitcast.69), calls=%async_computation | async-start | bytes 65536 | tf_op jit(solution)/shard_map/all_to_all | solution.py:101
  91.3 13.9 %copy-start = (f32[1,1024,400]{2,1,0:T(8,128)}, f32[1,1024,400]{2,1,0:T(8,128)S(1)}, u32[]{:S(2)}) copy-start(f32[1,1024,400]{2,1,0:T(8,128)S(1)} %copy.67) | copy-start | bytes 4915204
  98.0 7.2 copy-start.11
  105.2 80.2 %all-to-all-start.1 = ((bf16[64,40,400]{2,1,0:T(8,128)(2,1)}), bf16[64,40,400]{2,1,0:T(8,128)(2,1)S(1)}, u32[]{:S(2)}, u32[]{:S(2)}) async-start(bf16[64,40,400]{2,1,0:T(8,128)(2,1)} %bitcast.195), calls=%async_computation.1 | async-start | bytes 5242880 | tf_op jit(solution)/shard_map/all_to_all | solution.py:102
  132.1 50.0 %copy-start.18 = (s32[1,2,128]{2,1,0:T(2,128)S(1)}, s32[1,2,128]{2,1,0:T(2,128)}, u32[]{:S(2)}) copy-start(s32[1,2,128]{2,1,0:T(2,128)} %param.15) | copy-start | bytes 3076
  173.3 9.3 copy-start.15
  185.4 17.1 %copy-start.9 = (f32[128,200]{0,1:T(8,128)}, f32[128,200]{0,1:T(8,128)S(1)}, u32[]{:S(2)}) copy-start(f32[128,200]{0,1:T(8,128)S(1)} %copy.89) | copy-start | bytes 307204
  185.4 30.8 %all-to-all-start.3 = ((s32[64,1,40]{2,1,0:T(1,128)}), s32[64,1,40]{2,1,0:T(1,128)}, u32[]{:S(2)}, u32[]{:S(2)}) async-start(s32[64,1,40]{2,1,0:T(1,128)} %bitcast.146), calls=%async_computation.3 | async-start | bytes 65536 | tf_op jit(solution)/shard_map/all_to_all | solution.py:101
  201.0 1.6 copy-start.7
  204.6 0.9 copy-start.10
  216.2 11.8 %copy-start.12 = (s32[64,1,40]{2,1,0:T(1,128)S(1)}, s32[64,1,40]{2,1,0:T(1,128)}, u32[]{:S(2)}) copy-start(s32[64,1,40]{2,1,0:T(1,128)} %copy-done.11) | copy-start | bytes 30724
  216.2 71.3 %all-to-all-start.2 = ((bf16[64,40,400]{2,1,0:T(8,128)(2,1)}), bf16[64,40,400]{2,1,0:T(8,128)(2,1)S(1)}, u32[]{:S(2)}, u32[]{:S(2)}) async-start(bf16[64,40,400]{2,1,0:T(8,128)(2,1)} %bitcast.75), calls=%async_computation.2 | async-start | bytes 5242880 | tf_op jit(solution)/shard_map/all_to_all | solution.py:119
  287.6 1.5 copy-start.6
  306.9 1.4 copy-start.3
  306.9 1.3 copy-start.13
  306.9 2.4 copy-start.1
  318.4 297.3 %all-to-all-start.4 = ((bf16[64,40,400]{2,1,0:T(8,128)(2,1)}), bf16[64,40,400]{2,1,0:T(8,128)(2,1)}, u32[]{:S(2)}, u32[]{:S(2)}) async-start(bf16[64,40,400]{2,1,0:T(8,128)(2,1)} %bitcast.196), calls=%async_computation.4 | async-start | bytes 5242880 | tf_op jit(solution)/shard_map/all_to_all | solution.py:102
  326.4 281.0 %all-reduce.3.cloned.1.call-start = ((), (), s32[]{:S(2)}) async-start(), calls=%async_computation.6 | async-start | bytes 4096000 | tf_op jit(solution)/shard_map/psum | solution.py:128
  326.7 2.8 copy-start.19
  326.7 2.8 copy-start.16
  329.4 279.9 %copy-start.17 = (f32[1000]{0:T(1024)S(1)}, f32[1000]{0:T(1024)}, u32[]{:S(2)}) copy-start(f32[1000]{0:T(1024)} %param.11) | copy-start | bytes 12004
  607.4 2.2 copy-start.4
  623.9 2.0 copy-start.8
  642.2 297.7 %all-to-all-start.5 = ((bf16[64,40,400]{2,1,0:T(8,128)(2,1)}), bf16[64,40,400]{2,1,0:T(8,128)(2,1)}, u32[]{:S(2)}, u32[]{:S(2)}) async-start(bf16[64,40,400]{2,1,0:T(8,128)(2,1)} %bitcast.193), calls=%async_computation.5 | async-start | bytes 5242880 | tf_op jit(solution)/shard_map/all_to_all | solution.py:119
  650.7 280.6 %all-reduce.5.cloned.1.call-start = ((), (), s32[]{:S(2)}) async-start(), calls=%async_computation.7 | async-start | bytes 4096000 | tf_op jit(solution)/shard_map/psum | solution.py:128
  931.3 2.5 copy-start.5
  959.1 2.2 copy-start.2
Sparse Core Ops, SparseCore 0:
  332.6 274.6 all-reduce.2
  656.9 274.2 all-reduce.4
where the time goes:
time: 982 us; the launch traced here: 974 us
  waiting for transfers between devices  619 us (63%)
  other arithmetic  159 us (16%)
  local copies, waits for them, and re-layouts  117 us (12%)
  starting transfers between devices  56.3 us (6%)
  between operations  15.3 us (2%)
    psum x2, waiting for transfers between devices, shards(): relation_total = lax.psum(relation_local, ('edge', 'rep'))  554 us
    sub x2, other arithmetic, shards(): ranks = jnp.arange(request_count, dtype=jnp.int32) - starts[sorted_owner]  71.6 us
    all_to_all x2, waiting for transfers between devices, shards(): lax.all_to_all(send_grads, 'edge', split_axis=0, concat_axis=0, tiled=True)  58.7 us
    scatter-add x2, other arithmetic, shards(): jax.ops.segment_sum(returned.reshape(owners_count * capacity, width).asty...  37 us
    all_to_all x2, starting transfers between devices, shards(): lax.all_to_all(send_rows, 'edge', split_axis=0, concat_axis=0, tiled=True)  23 us
    scatter x2, local copies, waits for them, and re-layouts, shards(): send_grads = jnp.zeros((owners_count * capacity, width), jnp.bfloat16).at...  20.5 us
  transfers between devices with their start and end apart: 8, of which 4 were waited for; matrix products, arithmetic and copies ran while one was open for 12% of the time, Pallas kernels for 0%

commit v1 on v0

--- a/solution.py
+++ b/solution.py
@@ -125,7 +125,7 @@
         relation_local = jax.ops.segment_sum(
             relation_grads, relation_ids, num_segments=rel_table.shape[0]
         )
-        relation_total = lax.psum(relation_local, ("edge", "rep"))
+        relation_total = lax.psum(lax.psum(relation_local, "rep"), "edge")
         accum = accum + jnp.mean(entity_grad * entity_grad, axis=1)
         table = table - entity_rate * entity_grad / jnp.sqrt(accum)[:, None]
         rel_state = rel_state + jnp.mean(relation_total * relation_total, axis=1)

time: 982 us -> 941 us (0.958)
  waiting for transfers between devices: 619 us -> 578 us
    psum x2 -> x4, waiting for transfers between devices: 554 us -> 513 us  [shards(): relation_total = lax.psum(lax.psum(relation_local, 'rep'), 'edge')]
  transfers between devices with their start and end apart: 8 -> 10, of which waited for: 4 -> 6; matrix products, arithmetic and copies ran while one was open for 12% -> 13% of each run, Pallas kernels for 0% -> 0%
where the time goes in v1:
time: 941 us; the launch traced here: 932 us
  waiting for transfers between devices  578 us (61%)
  other arithmetic  159 us (17%)
  local copies, waits for them, and re-layouts  117 us (12%)
  starting transfers between devices  56.4 us (6%)
  between operations  15 us (2%)
    psum x4, waiting for transfers between devices, shards(): relation_total = lax.psum(lax.psum(relation_local, 'rep'), 'edge')  513 us
    sub x2, other arithmetic, shards(): ranks = jnp.arange(request_count, dtype=jnp.int32) - starts[sorted_owner]  71.6 us
    all_to_all x2, waiting for transfers between devices, shards(): lax.all_to_all(send_grads, 'edge', split_axis=0, concat_axis=0, tiled=True)  58.7 us
    scatter-add x2, other arithmetic, shards(): jax.ops.segment_sum(returned.reshape(owners_count * capacity, width).asty...  37 us
    all_to_all x2, starting transfers between devices, shards(): lax.all_to_all(send_rows, 'edge', split_axis=0, concat_axis=0, tiled=True)  23 us
    scatter x2, local copies, waits for them, and re-layouts, shards(): send_grads = jnp.zeros((owners_count * capacity, width), jnp.bfloat16).at...  20.5 us
    all_to_all x2, starting transfers between devices, shards(): lax.all_to_all(send_grads, 'edge', split_axis=0, concat_axis=0, tiled=True)  19 us
  transfers between devices with their start and end apart: 10, of which 6 were waited for; matrix products, arithmetic and copies ran while one was open for 13% of the time, Pallas kernels for 0%

profile of v1, /device:TPU:14, one launch (start us, length us, event | category | flops | bytes accessed | tf_op | source)
XLA Modules:
  0.0 932.3 jit_solution(8140970502717029525)
XLA Ops:
  12.8 5.0 sort.31
  17.9 7.1 gather_fusion
  25.0 4.5 fusion.62
  30.4 35.7 %select_subtract_fusion.1 = s32[1280]{0:T(1024)S(1)} fusion(pred[1280]{0:T(1024)(128)(4,1)S(1)} %get-tuple-element.137, pred[1280]{0:T(1024)(128)(4,1)S(1)} %get-tuple-element.136, pred[1280]{0:T(1024)(128)(4,1)S(1)} %get-tuple-element.135, pred[1280]{0:T(1024)(128)(4,1)S(1)} %get-tuple-element.134, pred[1280]{0:T(1024)(128)(4,1)S(1)} %get-tuple-element.133, ...), kind=kLoop, calls=%fused_computation.273 | loop fusion | flops 74240 | bytes 83428 | tf_op jit(solution)/shard_map/sub | solution.py:96
  66.1 5.2 scatter_custom_fusion
  71.4 5.3 scatter_custom_fusion.1
  77.3 12.1 %all-to-all-start = ((s32[64,1,40]{2,1,0:T(1,128)}), s32[64,1,40]{2,1,0:T(1,128)S(1)}, u32[]{:S(2)}, u32[]{:S(2)}) async-start(s32[64,1,40]{2,1,0:T(1,128)} %bitcast.69), calls=%async_computation | async-start | bytes 65536 | tf_op jit(solution)/shard_map/all_to_all | solution.py:101
  91.3 6.7 all-to-all-done
  98.1 7.1 gather_fusion.1
  105.2 6.2 all-to-all-start.1
  111.4 5.0 sort.32
  116.5 7.1 gather_fusion.4
  125.4 4.3 fusion.63
  132.1 35.9 %select_subtract_fusion = s32[1280]{0:T(1024)S(1)} fusion(pred[1280]{0:T(1024)(128)(4,1)S(1)} %get-tuple-element.80, pred[1280]{0:T(1024)(128)(4,1)S(1)} %get-tuple-element.79, pred[1280]{0:T(1024)(128)(4,1)S(1)} %get-tuple-element.78, pred[1280]{0:T(1024)(128)(4,1)S(1)} %get-tuple-element.77, pred[1280]{0:T(1024)(128)(4,1)S(1)} %get-tuple-element.76, ...), kind=kLoop, calls=%fused_computation.272 | loop fusion | flops 74240 | bytes 83428 | tf_op jit(solution)/shard_map/sub | solution.py:96
  168.0 5.2 scatter_custom_fusion.4
  173.3 5.3 scatter_custom_fusion.5
  185.4 10.9 %all-to-all-start.3 = ((s32[64,1,40]{2,1,0:T(1,128)}), s32[64,1,40]{2,1,0:T(1,128)}, u32[]{:S(2)}, u32[]{:S(2)}) async-start(s32[64,1,40]{2,1,0:T(1,128)} %bitcast.146), calls=%async_computation.3 | async-start | bytes 65536 | tf_op jit(solution)/shard_map/all_to_all | solution.py:101
  196.3 4.7 gather_fusion.2
  206.3 10.0 %scatter_custom_fusion.2 = bf16[2560,400]{1,0:T(8,128)(2,1)} fusion(s32[1280]{0:T(1024)} %copy-done.14, bf16[1280,400]{1,0:T(8,128)(2,1)S(1)} %copy.75, bf16[]{:T(256)} %constant.79.clone.1), kind=kCustom, calls=%fused_computation.34 | custom fusion | bytes 2048512 | tf_op jit(solution)/shard_map/scatter | solution.py:116
  216.2 10.5 %all-to-all-start.2 = ((bf16[64,40,400]{2,1,0:T(8,128)(2,1)}), bf16[64,40,400]{2,1,0:T(8,128)(2,1)S(1)}, u32[]{:S(2)}, u32[]{:S(2)}) async-start(bf16[64,40,400]{2,1,0:T(8,128)(2,1)} %bitcast.75), calls=%async_computation.2 | async-start | bytes 5242880 | tf_op jit(solution)/shard_map/all_to_all | solution.py:119
  228.9 58.7 %all-to-all-done.2 = bf16[64,40,400]{2,1,0:T(8,128)(2,1)S(1)} async-done(((bf16[64,40,400]{2,1,0:T(8,128)(2,1)}), bf16[64,40,400]{2,1,0:T(8,128)(2,1)S(1)}, u32[]{:S(2)}, u32[]{:S(2)}) %all-to-all-start.2) | async-done | bytes 2048032 | tf_op jit(solution)/shard_map/all_to_all | solution.py:119
  289.1 17.8 %scatter_custom_fusion.3 = f32[1024,400]{1,0:T(8,128)S(1)} fusion(s32[2560]{0:T(1024)S(1)} %reshape.707, bf16[2560,400]{1,0:T(8,128)(2,1)} %bitcast.194, f32[]{:T(128)} %constant.68.clone.1), kind=kCustom, calls=%fused_computation.20 | custom fusion | flops 2048000 | bytes 3686404 | tf_op jit(solution)/shard_map/scatter-add | solution.py:120
  311.3 7.1 gather_fusion.5
  318.4 8.0 all-to-all-start.4
  329.5 62.8 %all-reduce.5.cloned.1.call-done = f32[1000,400]{1,0:T(8,128)} async-done(((f32[1000,400]{1,0:T(8,128)}), f32[1000,400]{1,0:T(8,128)}) %all-reduce.5.cloned.1.call-update) | async-done | bytes 1600016 | tf_op jit(solution)/shard_map/psum | solution.py:128
  392.4 194.3 %all-reduce.7.cloned.1.call-done = f32[1000,400]{1,0:T(8,128)} async-done(((f32[1000,400]{1,0:T(8,128)}), f32[1000,400]{1,0:T(8,128)}) %all-reduce.7.cloned.1.call-update) | async-done | bytes 1600016 | tf_op jit(solution)/shard_map/psum | solution.py:128
  595.0 6.9 gather_fusion.6
  611.0 10.6 %scatter_custom_fusion.7 = bf16[2560,400]{1,0:T(8,128)(2,1)} fusion(s32[1280]{0:T(1024)S(1)} %copy-done.16, bf16[1280,400]{1,0:T(8,128)(2,1)} %copy.84, bf16[]{:T(256)} %constant.79.clone.1), kind=kCustom, calls=%fused_computation.32 | custom fusion | bytes 2048512 | tf_op jit(solution)/shard_map/scatter | solution.py:116
  621.6 8.5 all-to-all-start.5
  633.2 62.8 %all-reduce.9.cloned.1.call-done = f32[1000,400]{1,0:T(8,128)} async-done(((f32[1000,400]{1,0:T(8,128)}), f32[1000,400]{1,0:T(8,128)}) %all-reduce.9.cloned.1.call-update) | async-done | bytes 1600016 | tf_op jit(solution)/shard_map/psum | solution.py:128
  697.6 192.6 %all-reduce.11.cloned.1.call-done = f32[1000,400]{1,0:T(8,128)} async-done(((f32[1000,400]{1,0:T(8,128)}), f32[1000,400]{1,0:T(8,128)}) %all-reduce.11.cloned.1.call-update) | async-done | bytes 1600016 | tf_op jit(solution)/shard_map/psum | solution.py:128
  898.8 19.2 %scatter_custom_fusion.8 = f32[1024,400]{1,0:T(8,128)} fusion(s32[2560]{0:T(1024)S(1)} %reshape.747, bf16[2560,400]{1,0:T(8,128)(2,1)} %bitcast.160, f32[]{:T(128)} %constant.68.clone.1), kind=kCustom, calls=%fused_computation.18 | custom fusion | flops 2048000 | bytes 3686404 | tf_op jit(solution)/shard_map/scatter-add | solution.py:120
  (172 shorter events, 74.4 us)
Async XLA Ops:
  71.4 114.0 %copy-start.14 = (s32[1280]{0:T(1024)}, s32[1280]{0:T(1024)S(1)}, u32[]{:S(2)}) copy-start(s32[1280]{0:T(1024)S(1)} %compare_select_fusion.6) | copy-start | bytes 15364
  77.3 20.6 %all-to-all-start = ((s32[64,1,40]{2,1,0:T(1,128)}), s32[64,1,40]{2,1,0:T(1,128)S(1)}, u32[]{:S(2)}, u32[]{:S(2)}) async-start(s32[64,1,40]{2,1,0:T(1,128)} %bitcast.69), calls=%async_computation | async-start | bytes 65536 | tf_op jit(solution)/shard_map/all_to_all | solution.py:101
  91.3 13.9 %copy-start = (f32[1,1024,400]{2,1,0:T(8,128)}, f32[1,1024,400]{2,1,0:T(8,128)S(1)}, u32[]{:S(2)}) copy-start(f32[1,1024,400]{2,1,0:T(8,128)S(1)} %copy.67) | copy-start | bytes 4915204
  98.0 7.2 copy-start.11
  105.2 80.2 %all-to-all-start.1 = ((bf16[64,40,400]{2,1,0:T(8,128)(2,1)}), bf16[64,40,400]{2,1,0:T(8,128)(2,1)S(1)}, u32[]{:S(2)}, u32[]{:S(2)}) async-start(bf16[64,40,400]{2,1,0:T(8,128)(2,1)} %bitcast.195), calls=%async_computation.1 | async-start | bytes 5242880 | tf_op jit(solution)/shard_map/all_to_all | solution.py:102
  132.1 50.0 %copy-start.18 = (s32[1,2,128]{2,1,0:T(2,128)S(1)}, s32[1,2,128]{2,1,0:T(2,128)}, u32[]{:S(2)}) copy-start(s32[1,2,128]{2,1,0:T(2,128)} %param.15) | copy-start | bytes 3076
  173.3 9.3 copy-start.15
  185.4 17.1 %copy-start.9 = (f32[128,200]{0,1:T(8,128)}, f32[128,200]{0,1:T(8,128)S(1)}, u32[]{:S(2)}) copy-start(f32[128,200]{0,1:T(8,128)S(1)} %copy.89) | copy-start | bytes 307204
  185.4 30.8 %all-to-all-start.3 = ((s32[64,1,40]{2,1,0:T(1,128)}), s32[64,1,40]{2,1,0:T(1,128)}, u32[]{:S(2)}, u32[]{:S(2)}) async-start(s32[64,1,40]{2,1,0:T(1,128)} %bitcast.146), calls=%async_computation.3 | async-start | bytes 65536 | tf_op jit(solution)/shard_map/all_to_all | solution.py:101
  201.0 1.6 copy-start.7
  204.6 0.9 copy-start.10
  216.2 11.8 %copy-start.12 = (s32[64,1,40]{2,1,0:T(1,128)S(1)}, s32[64,1,40]{2,1,0:T(1,128)}, u32[]{:S(2)}) copy-start(s32[64,1,40]{2,1,0:T(1,128)} %copy-done.11) | copy-start | bytes 30724
  216.2 71.3 %all-to-all-start.2 = ((bf16[64,40,400]{2,1,0:T(8,128)(2,1)}), bf16[64,40,400]{2,1,0:T(8,128)(2,1)S(1)}, u32[]{:S(2)}, u32[]{:S(2)}) async-start(bf16[64,40,400]{2,1,0:T(8,128)(2,1)} %bitcast.75), calls=%async_computation.2 | async-start | bytes 5242880 | tf_op jit(solution)/shard_map/all_to_all | solution.py:119
  287.6 1.5 copy-start.6
  306.9 1.4 copy-start.3
  306.9 1.3 copy-start.13
  306.9 2.4 copy-start.1
  318.4 276.6 %all-to-all-start.4 = ((bf16[64,40,400]{2,1,0:T(8,128)(2,1)}), bf16[64,40,400]{2,1,0:T(8,128)(2,1)}, u32[]{:S(2)}, u32[]{:S(2)}) async-start(bf16[64,40,400]{2,1,0:T(8,128)(2,1)} %bitcast.196), calls=%async_computation.4 | async-start | bytes 5242880 | tf_op jit(solution)/shard_map/all_to_all | solution.py:102
  326.4 65.9 %all-reduce.5.cloned.1.call-start = ((), (), s32[]{:S(2)}) async-start(), calls=%async_computation.6 | async-start | bytes 4096000 | tf_op jit(solution)/shard_map/psum | solution.py:128
  329.5 62.9 %copy-start.19 = (s32[128]{0:T(128)S(1)}, s32[128]{0:T(128)}, u32[]{:S(2)}) copy-start(s32[128]{0:T(128)} %get-tuple-element.191) | copy-start | bytes 1540
  329.5 62.9 %copy-start.16 = (s32[1280]{0:T(1024)S(1)}, s32[1280]{0:T(1024)}, u32[]{:S(2)}) copy-start(s32[1280]{0:T(1024)} %copy-done.15) | copy-start | bytes 15364
  329.5 257.3 %all-reduce.7.cloned.1.call-start = ((), (), s32[]{:S(2)}) async-start(), calls=%async_computation.7 | async-start | bytes 4096000 | tf_op jit(solution)/shard_map/psum | solution.py:128
  392.3 196.4 %copy-start.17 = (f32[1000]{0:T(1024)S(1)}, f32[1000]{0:T(1024)}, u32[]{:S(2)}) copy-start(f32[1000]{0:T(1024)} %param.11) | copy-start | bytes 12004
  586.8 2.2 copy-start.4
  603.2 2.0 copy-start.8
  621.6 277.2 %all-to-all-start.5 = ((bf16[64,40,400]{2,1,0:T(8,128)(2,1)}), bf16[64,40,400]{2,1,0:T(8,128)(2,1)}, u32[]{:S(2)}, u32[]{:S(2)}) async-start(bf16[64,40,400]{2,1,0:T(8,128)(2,1)} %bitcast.193), calls=%async_computation.5 | async-start | bytes 5242880 | tf_op jit(solution)/shard_map/all_to_all | solution.py:119
  630.1 65.9 %all-reduce.9.cloned.1.call-start = ((), (), s32[]{:S(2)}) async-start(), calls=%async_computation.8 | async-start | bytes 4096000 | tf_op jit(solution)/shard_map/psum | solution.py:128
  633.1 257.0 %all-reduce.11.cloned.1.call-start = ((), (), s32[]{:S(2)}) async-start(), calls=%async_computation.9 | async-start | bytes 4096000 | tf_op jit(solution)/shard_map/psum | solution.py:128
  890.2 2.5 copy-start.5
  918.0 2.2 copy-start.2
Sparse Core Ops, SparseCore 0:
  329.6 62.6 all-reduce.4
  396.2 190.5 all-reduce.6
  633.4 62.4 all-reduce.8
  699.3 190.8 all-reduce.10
